TPU v7x, 256 devices: a whole 4x4x8 slice. The times are simulated.
256 devices in a mesh: blk: 64 (over z, y, x_hi), grp: 4 (over x_lo, core).
Axes of the slice: x: 4 (x_hi: 2, x_lo: 2; x = x_hi * 2 + x_lo), y: 4, z: 8, core: 2. Of those that a mesh axis runs over, the one named last changes fastest.
Arguments:
- embeddings: float32 [98304, 1024], P(('blk', 'grp')), may hold values from -0.25 to 0.25
- normalizers: bfloat16 [98304], P(('blk', 'grp')), may hold values from 2 to 5
- partner_index: int32 [98304], P(('blk', 'grp')), may hold values from 0 to 98303, as said below
Outputs:
- grad_embeddings: float32 [98304, 1024], P(('blk', 'grp'))
Inputs may be any that keep to these rules, and one draw needn't show every extreme that they name: partner_index[partner_index[i]] = i and partner_index[i] != i; each view's partner lies in the same row block of 1536 views (same i // 1536).
All inputs are finite; a program needn't handle non-finite values.
Results may differ from a plain program's by a relative error of at most 0.0046.
Values may be sent and summed in bfloat16 or wider, within the bound.
A program may use at most 128 MiB of HBM per device.

v0:
```python
import jax
import jax.numpy as jnp
from jax import lax
from jax.sharding import PartitionSpec as P

ROUNDS = 2


inverse_temp = 10.0


def from_behind(x, axis, by):
    devices = lax.axis_size(axis)
    return lax.ppermute(x, axis, [(i, (i + by) % devices) for i in range(devices)])


def pair_weights(scores, left_norm, right_norm):
    return (jnp.exp(scores - left_norm[:, None]) + jnp.exp(scores - right_norm[None, :])).astype(
        jnp.bfloat16
    )


def per_device(embeddings, normalizers, partner_index):
    inv_norm = lax.rsqrt(jnp.sum(embeddings * embeddings, axis=1, keepdims=True) + 1e-06)
    normed = embeddings * inv_norm
    rounded = normed.astype(jnp.bfloat16)
    row_count = embeddings.shape[0]
    block_rows = row_count * lax.axis_size("grp")
    own_units, own_norms = (
        lax.all_gather(rounded, "grp", axis=0, tiled=True),
        lax.all_gather(normalizers, "grp", axis=0, tiled=True),
    )
    resident_norm = normalizers.astype(jnp.float32)
    pulled = jnp.zeros(embeddings.shape, jnp.float32)
    offsets = list(range(1, ROUNDS + 1))
    offsets = offsets + list(range(-ROUNDS, 0))
    for offset in offsets:
        guests, guest_norms = from_behind((own_units, own_norms), "blk", offset)
        scores = (
            lax.dot_general(
                rounded, guests, (((1,), (1,)), ((), ())), preferred_element_type=jnp.float32
            )
            * inverse_temp
        )
        weights = pair_weights(scores, resident_norm, guest_norms.astype(jnp.float32))
        pulled = pulled + jnp.dot(weights, guests, preferred_element_type=jnp.float32)
    local_index = partner_index - lax.axis_index("blk") * block_rows
    positive = jnp.take(own_units, local_index, axis=0).astype(jnp.float32)
    grad_unit = inverse_temp * (pulled - 2.0 * positive)
    radial = jnp.sum(normed * grad_unit, axis=1, keepdims=True)
    return inv_norm * (grad_unit - normed * radial)


def solution(mesh):
    placed = (P(("blk", "grp"), None), P(("blk", "grp")), P(("blk", "grp")))
    return jax.shard_map(
        per_device, mesh=mesh, in_specs=placed, out_specs=P(("blk", "grp"), None), check_vma=False
    )
```

profile of v0, /device:TPU:28, one launch (start us, length us, event | category | flops | bytes accessed | tf_op | source)
XLA Modules:
  0.0 320.9 jit_solution(16335163028028469468)
XLA Ops:
  6.5 0.0 all-gather.3.cloned.1.call-start
  6.5 1.7 multiply_reduce_fusion.1
  8.3 0.2 copy-done
  8.4 1.0 multiply_convert_fusion
  9.4 0.0 all-gather.3.cloned.1.call-update
  9.5 42.5 %all-gather.3.cloned.1.call-done = bf16[1536,1024]{1,0:T(8,128)(2,1)} async-done(((bf16[384,1024]{1,0:T(8,128)(2,1)}), bf16[1536,1024]{1,0:T(8,128)(2,1)}) %all-gather.3.cloned.1.call-update) | async-done | bytes 3145744 | tf_op jit(solution)/shard_map/all_gather | solution.py:30
  52.0 1.8 collective-permute-start
  53.8 1.5 collective-permute-start.2
  55.2 0.5 collective-permute-start.4
  55.8 1.8 collective-permute-start.6
  57.5 0.0 copy-done.2
  57.6 196.5 %all-gather = bf16[4,1,384]{2,1,0:T(2,128)(2,1)S(1)} all-gather(bf16[1,1,384]{2,1,0:T(2,128)(2,1)S(1)} %reshape.26), channel_id=1, replica_groups=mesh['blk'=64,'grp'=4] {'grp'}, dimensions={0}, use_global_device_ids=true | all-gather | bytes 3840 | tf_op jit(solution)/shard_map/all_gather | solution.py:31
  254.1 0.1 collective-permute-start.1
  254.2 5.1 %collective-permute-done.1 = bf16[1536]{0:T(1024)(128)(2,1)S(1)} collective-permute-done((bf16[1536]{0:T(1024)(128)(2,1)S(1)}, bf16[1536]{0:T(1024)(128)(2,1)S(1)}, u32[]{:S(2)}, u32[]{:S(2)}) %collective-permute-start.1) | collective-permute-done | bytes 3104 | tf_op jit(solution)/shard_map/ppermute | solution.py:14
  259.3 0.0 collective-permute-start.3
  259.3 3.6 %collective-permute-done.3 = bf16[1536]{0:T(1024)(128)(2,1)S(1)} collective-permute-done((bf16[1536]{0:T(1024)(128)(2,1)S(1)}, bf16[1536]{0:T(1024)(128)(2,1)S(1)}, u32[]{:S(2)}, u32[]{:S(2)}) %collective-permute-start.3) | collective-permute-done | bytes 3104 | tf_op jit(solution)/shard_map/ppermute | solution.py:14
  262.9 0.0 collective-permute-start.5
  262.9 0.0 copy-done.3
  262.9 5.7 %collective-permute-done.5 = bf16[1536]{0:T(1024)(128)(2,1)S(1)} collective-permute-done((bf16[1536]{0:T(1024)(128)(2,1)S(1)}, bf16[1536]{0:T(1024)(128)(2,1)S(1)}, u32[]{:S(2)}, u32[]{:S(2)}) %collective-permute-start.5) | collective-permute-done | bytes 3104 | tf_op jit(solution)/shard_map/ppermute | solution.py:14
  268.6 1.6 collective-permute-start.7
  270.2 6.5 %collective-permute-done.7 = bf16[1536]{0:T(1024)(128)(2,1)S(1)} collective-permute-done((bf16[1536]{0:T(1024)(128)(2,1)S(1)}, bf16[1536]{0:T(1024)(128)(2,1)S(1)}, u32[]{:S(2)}, u32[]{:S(2)}) %collective-permute-start.7) | collective-permute-done | bytes 3104 | tf_op jit(solution)/shard_map/ppermute | solution.py:14
  276.7 5.1 %gather_fusion = bf16[384,1024]{1,0:T(8,128)(2,1)S(1)} fusion(bf16[1536,1024]{1,0:T(8,128)(2,1)} %all-gather.3.cloned.1.call-done, s32[1024]{0:T(1024)S(1)} %pad_clamp_fusion), kind=kCustom, calls=%fused_computation | custom fusion | bytes 1574400 | tf_op jit(solution)/shard_map/jit(_take)/gather | solution.py:48
  281.8 0.0 collective-permute-done
  281.9 0.0 copy-done.1
  281.9 6.9 %fusion = f32[384,1024]{1,0:T(8,128)} fusion(bf16[1536,1024]{1,0:T(8,128)(2,1)} %collective-permute-done, bf16[384,1024]{1,0:T(8,128)(2,1)S(1)} %copy-done.1, f32[1536]{0:T(1024)S(1)} %convert_element_type.35, f32[384]{0:T(512)S(1)} %convert_element_type.34), kind=kOutput, calls=%fused_computation.14 | convolution fusion | flops 2418868224 | bytes 5512704 | tf_op jit(solution)/shard_map/dot_general | solution.py:46
  288.8 0.0 collective-permute-done.2
  288.8 6.9 %fusion.1 = f32[384,1024]{1,0:T(8,128)} fusion(bf16[1536,1024]{1,0:T(8,128)(2,1)} %collective-permute-done.2, bf16[384,1024]{1,0:T(8,128)(2,1)S(1)} %copy-done.1, f32[1536]{0:T(1024)S(1)} %convert_element_type.37, f32[384]{0:T(512)S(1)} %convert_element_type.34), kind=kOutput, calls=%fused_computation.15 | convolution fusion | flops 2418868224 | bytes 5512704 | tf_op jit(solution)/shard_map/dot_general | solution.py:46
  295.7 0.0 collective-permute-done.4
  295.7 6.9 %fusion.2 = f32[384,1024]{1,0:T(8,128)} fusion(bf16[1536,1024]{1,0:T(8,128)(2,1)} %collective-permute-done.4, bf16[384,1024]{1,0:T(8,128)(2,1)S(1)} %copy-done.1, f32[1536]{0:T(1024)S(1)} %convert_element_type.39, f32[384]{0:T(512)S(1)} %convert_element_type.34), kind=kOutput, calls=%fused_computation.16 | convolution fusion | flops 2418868224 | bytes 5512704 | tf_op jit(solution)/shard_map/dot_general | solution.py:46
  302.6 0.0 collective-permute-done.6
  302.6 8.6 %multiply_reduce_fusion = (f32[384]{0:T(512)S(1)}, f32[384,1024]{1,0:T(8,128)}) fusion(f32[384,1024]{1,0:T(8,128)S(1)} %copy-done, f32[384]{0:T(512)S(1)} %add_rsqrt_fusion, bf16[384,1024]{1,0:T(8,128)(2,1)S(1)} %gather_fusion, pred[384]{0:T(512)(128)(4,1)S(1)} %get-tuple-element.5, bf16[1536,1024]{1,0:T(8,128)(2,1)} %collective-permute-done.6, ...), kind=kOutput, calls=%fused_computation.10 | convolution fusion | flops 2423193088 | bytes 12594048 | tf_op jit(solution)/shard_map/dot_general | solution.py:46
  311.2 2.8 subtract_multiply_fusion
  (15 shorter events, 0.1 us)
Async XLA Ops:
  6.5 1.9 copy-start
  6.5 51.0 %copy-start.2 = (bf16[384]{0:T(512)(128)(2,1)S(1)}, bf16[384]{0:T(512)(128)(2,1)}, u32[]{:S(2)}) copy-start(bf16[384]{0:T(512)(128)(2,1)} %param.4) | copy-start | bytes 2308
  6.5 256.3 %copy-start.3 = (s32[384]{0:T(512)S(1)}, s32[384]{0:T(512)}, u32[]{:S(2)}) copy-start(s32[384]{0:T(512)} %param.5) | copy-start | bytes 4612
  6.5 45.4 %all-gather.3.cloned.1.call-start = ((), (), s32[]{:S(2)}) async-start(), calls=%async_computation | async-start | bytes 3932160 | tf_op jit(solution)/shard_map/all_gather | solution.py:30
  52.0 229.9 %collective-permute-start = (bf16[1536,1024]{1,0:T(8,128)(2,1)}, bf16[1536,1024]{1,0:T(8,128)(2,1)}, u32[]{:S(2)}, u32[]{:S(2)}) collective-permute-start(bf16[1536,1024]{1,0:T(8,128)(2,1)} %all-gather.3.cloned.1.call-done), channel_id=1, source_target_pairs={{0,4},{4,8},{8,12},{12,16},{16,20},{20,24},{24,28},{28,32},{32,36}... | collective-permute-start | bytes 9437192 | tf_op jit(solution)/shard_map/ppermute | solution.py:14
  53.8 235.0 %collective-permute-start.2 = (bf16[1536,1024]{1,0:T(8,128)(2,1)}, bf16[1536,1024]{1,0:T(8,128)(2,1)}, u32[]{:S(2)}, u32[]{:S(2)}) collective-permute-start(bf16[1536,1024]{1,0:T(8,128)(2,1)} %all-gather.3.cloned.1.call-done), channel_id=1, source_target_pairs={{0,8},{4,12},{8,16},{12,20},{16,24},{20,28},{24,32},{28,36},{32,40... | collective-permute-start | bytes 9437192 | tf_op jit(solution)/shard_map/ppermute | solution.py:14
  55.2 240.4 %collective-permute-start.4 = (bf16[1536,1024]{1,0:T(8,128)(2,1)}, bf16[1536,1024]{1,0:T(8,128)(2,1)}, u32[]{:S(2)}, u32[]{:S(2)}) collective-permute-start(bf16[1536,1024]{1,0:T(8,128)(2,1)} %all-gather.3.cloned.1.call-done), channel_id=1, source_target_pairs={{0,248},{4,252},{8,0},{12,4},{16,8},{20,12},{24,16},{28,20},{32,24... | collective-permute-start | bytes 9437192 | tf_op jit(solution)/shard_map/ppermute | solution.py:14
  55.8 246.8 %collective-permute-start.6 = (bf16[1536,1024]{1,0:T(8,128)(2,1)}, bf16[1536,1024]{1,0:T(8,128)(2,1)}, u32[]{:S(2)}, u32[]{:S(2)}) collective-permute-start(bf16[1536,1024]{1,0:T(8,128)(2,1)} %all-gather.3.cloned.1.call-done), channel_id=1, source_target_pairs={{0,252},{4,0},{8,4},{12,8},{16,12},{20,16},{24,20},{28,24},{32,28}... | collective-permute-start | bytes 9437192 | tf_op jit(solution)/shard_map/ppermute | solution.py:14
  254.1 5.2 %collective-permute-start.1 = (bf16[1536]{0:T(1024)(128)(2,1)S(1)}, bf16[1536]{0:T(1024)(128)(2,1)S(1)}, u32[]{:S(2)}, u32[]{:S(2)}) collective-permute-start(bf16[1536]{0:T(1024)(128)(2,1)S(1)} %reshape.27), channel_id=1, source_target_pairs={{0,4},{4,8},{8,12},{12,16},{16,20},{20,24},{24,28},{28,32},{32,36}... | collective-permute-start | bytes 9224 | tf_op jit(solution)/shard_map/ppermute | solution.py:14
  259.3 3.6 %collective-permute-start.3 = (bf16[1536]{0:T(1024)(128)(2,1)S(1)}, bf16[1536]{0:T(1024)(128)(2,1)S(1)}, u32[]{:S(2)}, u32[]{:S(2)}) collective-permute-start(bf16[1536]{0:T(1024)(128)(2,1)S(1)} %reshape.27), channel_id=1, source_target_pairs={{0,8},{4,12},{8,16},{12,20},{16,24},{20,28},{24,32},{28,36},{32,40... | collective-permute-start | bytes 9224 | tf_op jit(solution)/shard_map/ppermute | solution.py:14
  262.9 5.7 %collective-permute-start.5 = (bf16[1536]{0:T(1024)(128)(2,1)S(1)}, bf16[1536]{0:T(1024)(128)(2,1)S(1)}, u32[]{:S(2)}, u32[]{:S(2)}) collective-permute-start(bf16[1536]{0:T(1024)(128)(2,1)S(1)} %reshape.27), channel_id=1, source_target_pairs={{0,248},{4,252},{8,0},{12,4},{16,8},{20,12},{24,16},{28,20},{32,24... | collective-permute-start | bytes 9224 | tf_op jit(solution)/shard_map/ppermute | solution.py:14
  268.6 8.1 %collective-permute-start.7 = (bf16[1536]{0:T(1024)(128)(2,1)S(1)}, bf16[1536]{0:T(1024)(128)(2,1)S(1)}, u32[]{:S(2)}, u32[]{:S(2)}) collective-permute-start(bf16[1536]{0:T(1024)(128)(2,1)S(1)} %reshape.27), channel_id=1, source_target_pairs={{0,252},{4,0},{8,4},{12,8},{16,12},{20,16},{24,20},{28,24},{32,28}... | collective-permute-start | bytes 9224 | tf_op jit(solution)/shard_map/ppermute | solution.py:14
  276.7 5.2 %copy-start.1 = (bf16[384,1024]{1,0:T(8,128)(2,1)S(1)}, bf16[384,1024]{1,0:T(8,128)(2,1)}, u32[]{:S(2)}) copy-start(bf16[384,1024]{1,0:T(8,128)(2,1)} %multiply_convert_fusion) | copy-start | bytes 2359300
Sparse Core Ops, SparseCore 0:
  9.6 42.3 all-gather.2
where the time goes:
time: 321 us
  blocking collectives  196 us (61%)
  waiting for transfers between devices  63.5 us (20%)
  matrix products  29.3 us (9%)
  between operations  13.5 us (4%)
  starting transfers between devices  7.19 us (2%)
  other arithmetic  5.65 us (2%)
  local copies, waits for them, and re-layouts  5.32 us (2%)
    all_gather x1, blocking collectives, per_device(): lax.all_gather(normalizers, 'grp', axis=0, tiled=True)  196 us
    all_gather x1, waiting for transfers between devices, per_device(): lax.all_gather(rounded, 'grp', axis=0, tiled=True)  42.5 us
    dot_general x4, matrix products, per_device(): jnp.dot(weights, guests, preferred_element_type=jnp.float32)  29.3 us
    ppermute x8, waiting for transfers between devices, from_behind(): lax.ppermute(x, axis, [(i, (i + by) % devices) for i in range(devices)])  20.9 us
    ppermute x8, starting transfers between devices, from_behind(): lax.ppermute(x, axis, [(i, (i + by) % devices) for i in range(devices)])  7.19 us
  transfers between devices with their start and end apart: 9, of which 5 were waited for; matrix products, arithmetic and copies ran while one was open for 8% of the time, Pallas kernels for 0%

commit v1 on v0

v1 whole, which is shorter than its diff:
```python
import functools

import jax
import jax.numpy as jnp
from jax import lax
from jax.experimental import pallas as pl
from jax.experimental.pallas import tpu as pltpu
from jax.sharding import PartitionSpec as P

MESH = pl.DeviceIdType.MESH
ROWS = 384
D = 1024
K = 6
R = ROWS // K
T = 128
TILES = ROWS // T
INV_TEMP = 10.0
SCALE = INV_TEMP * 1.4426950408889634


def tile_of(row):
    pieces = [row[:, k * R : (k + 1) * R] for k in range(K)]
    body = jnp.concatenate(pieces + [jnp.zeros((8 - K, R), row.dtype)], axis=0)
    return jnp.concatenate([body, jnp.zeros((8, 128 - R), row.dtype)], axis=1)


def columns_of(tile):
    turned = jnp.transpose(jnp.concatenate([tile] * 16, axis=0))
    return jnp.concatenate(
        [jnp.broadcast_to(turned[0:R, k : k + 1], (R, 128)) for k in range(K)], axis=0
    )


def kernel(
    blocks, emb_hbm, norm_ref, partner_ref, out_ref,
    emb, invs, block, ga, gb, relay, acc_own, acc_pair, part_out, part_in,
    e_own, e_pair, e_a, e_relay, e_b, col_own, col_pair,
    emb_sem, sib_s, sib_r, own_s, own_r, siba_s, siba_r, fwd_s, fwd_r, rel_s, rel_r,
    out_s, out_r, sibb_s, sibb_r, part_s, part_r, e_s, e_r,
):
    blk = lax.axis_index("blk")
    grp = lax.axis_index("grp")
    x_hi = blk % 2
    x_lo = grp // 2
    core = grp % 2
    turn = 2 * (1 - 2 * x_hi)
    pair_grp = (1 - x_lo) * 2 + core
    sib = (blk, x_lo * 2 + 1 - core)
    pair = (blk, pair_grp)
    outer = (blk + 1 - 2 * x_hi, pair_grp)
    ahead = ((blk + turn + blocks) % blocks, grp)
    behind = ((blk - turn + blocks) % blocks, grp)

    def remote(src, dst, send, recv, to):
        return pltpu.make_async_remote_copy(
            src_ref=src, dst_ref=dst, send_sem=send, recv_sem=recv, device_id=to, device_id_type=MESH
        )

    load = pltpu.make_async_copy(emb_hbm, emb, emb_sem)
    load.start()
    barrier = pltpu.get_barrier_semaphore()
    neighbours = (sib, pair, outer, ahead, behind)
    for to in neighbours:
        pl.semaphore_signal(barrier, inc=1, device_id=to, device_id_type=MESH)

    e_tile = tile_of(jnp.exp(-norm_ref[...].astype(jnp.float32)))
    e_own[...] = e_tile
    col_own[...] = columns_of(e_tile)
    load.wait()

    def normalize(t, _):
        at = pl.ds(pl.multiple_of(t * R, R), R)
        x = emb[at, :]
        inv = lax.rsqrt(jnp.sum(x * x, axis=1, keepdims=True) + 1e-06)
        invs[at, :] = jnp.broadcast_to(inv, (R, 128))
        block[grp, at, :] = (x * inv).astype(jnp.bfloat16)
        acc_own[at, :] = jnp.zeros((R, D), jnp.float32)
        acc_pair[at, :] = jnp.zeros((R, D), jnp.float32)
        return 0

    lax.fori_loop(0, K, normalize, 0)
    pl.semaphore_wait(barrier, len(neighbours))

    def lane_a(c, stream, n=1):
        return pl.ds(pl.multiple_of((c * 3 + stream) * R, R), n * R)

    def lane_b(c, stream, n=1):
        return pl.ds(pl.multiple_of((c * 2 + stream) * R, R), n * R)

    def piece(k):
        return pl.ds(pl.multiple_of(k * R, R), R)

    e_copies = [
        remote(e_own, e_pair, e_s.at[0], e_r.at[0], pair),
        remote(e_own, e_a.at[core, 0], e_s.at[1], e_r.at[1], outer),
        remote(e_own, e_a.at[core, 1], e_s.at[2], e_r.at[2], behind),
        remote(e_own, e_a.at[core, 2], e_s.at[3], e_r.at[3], ahead),
    ]
    e_sib = remote(e_a.at[core], e_a.at[core], e_s.at[4], e_r.at[4], sib)
    e_sib_in = remote(e_a.at[1 - core], e_a.at[1 - core], e_s.at[4], e_r.at[4], sib)
    e_fwd = remote(e_a.at[core, 0], e_b.at[core, 0], e_s.at[5], e_r.at[5], ahead)
    e_rel = remote(e_pair, e_relay, e_s.at[6], e_r.at[6], behind)
    e_out = remote(e_relay, e_b.at[core, 1], e_s.at[7], e_r.at[7], outer)
    e_sibb = remote(e_b.at[core], e_b.at[core], e_s.at[8], e_r.at[8], sib)
    e_sibb_in = remote(e_b.at[1 - core], e_b.at[1 - core], e_s.at[8], e_r.at[8], sib)

    def own_pair(k):
        return remote(block.at[grp, piece(k)], block.at[grp, piece(k)], own_s.at[0, k], own_r.at[0, k], pair)

    def pair_in(k):
        at = block.at[pair_grp, piece(k)]
        return remote(at, at, own_s.at[0, k], own_r.at[0, k], pair)

    def own_to(k, stream, to):
        return remote(
            block.at[grp, piece(k)], ga.at[k, lane_a(core, stream)],
            own_s.at[1 + stream, k], own_r.at[1 + stream, k], to,
        )

    def sib_a(k):
        at = ga.at[k, lane_a(core, 0, 3)]
        return remote(at, at, siba_s.at[k], siba_r.at[k], sib)

    def sib_a_in(k):
        at = ga.at[k, lane_a(1 - core, 0, 3)]
        return remote(at, at, siba_s.at[k], siba_r.at[k], sib)

    def fwd(k):
        return remote(ga.at[k, lane_a(core, 0)], gb.at[k, lane_b(core, 0)], fwd_s.at[k], fwd_r.at[k], ahead)

    def rel(k):
        return remote(block.at[pair_grp, piece(k)], relay.at[k], rel_s.at[k], rel_r.at[k], behind)

    def rel_out(k):
        return remote(relay.at[k], gb.at[k, lane_b(core, 1)], out_s.at[k], out_r.at[k], outer)

    def sib_b(k):
        at = gb.at[k, lane_b(core, 0, 2)]
        return remote(at, at, sibb_s.at[k], sibb_r.at[k], sib)

    def sib_b_in(k):
        at = gb.at[k, lane_b(1 - core, 0, 2)]
        return remote(at, at, sibb_s.at[k], sibb_r.at[k], sib)

    def tile(t):
        return pl.ds(pl.multiple_of(t * T, T), T)

    def partial(t):
        return remote(part_out.at[tile(t)], part_in.at[tile(t)], part_s.at[t], part_r.at[t], pair)

    sib_own = remote(block.at[grp], block.at[grp], sib_s.at[0], sib_r.at[0], sib)
    sib_own_in = remote(block.at[sib[1]], block.at[sib[1]], sib_s.at[0], sib_r.at[0], sib)
    sib_pair = remote(block.at[pair_grp], block.at[pair_grp], sib_s.at[1], sib_r.at[1], sib)
    cross = (1 - x_lo) * 2 + 1 - core
    sib_pair_in = remote(block.at[cross], block.at[cross], sib_s.at[1], sib_r.at[1], sib)

    for copy in e_copies:
        copy.start()

    def send_own(k, _):
        own_pair(k).start()
        own_to(k, 0, outer).start()
        own_to(k, 1, behind).start()
        own_to(k, 2, ahead).start()
        return 0

    lax.fori_loop(0, K, send_own, 0)
    sib_own.start()

    for copy in e_copies:
        copy.wait_recv()
    e_sib.start()
    e_fwd.start()
    e_rel.start()
    col_pair[...] = columns_of(e_pair[...])
    e_sib_in.wait_recv()

    def pull(rows, col, guests, e_row):
        scores = lax.dot_general(
            rows, guests, (((1,), (1,)), ((), ())), preferred_element_type=jnp.float32
        )
        spread = jnp.concatenate([col] * (guests.shape[0] // 128), axis=1)
        weights = (jnp.exp2(scores * SCALE) * (spread + e_row)).astype(jnp.bfloat16)
        return jnp.dot(weights, guests, preferred_element_type=jnp.float32)

    def e_row_of(e, k, streams):
        return jnp.concatenate(
            [e[c, s, pl.ds(k, 1), 0:R] for c in range(2) for s in range(streams)], axis=1
        )

    def pair_job(t, k):
        acc_pair[tile(t), :] += pull(
            block[pair_grp, tile(t), :], col_pair[tile(t), :], ga[k], e_row_of(e_a, k, 3)
        )

    def send_partial(t):
        part_out[tile(t), :] = acc_pair[tile(t), :].astype(jnp.bfloat16)
        partial(t).start()

    def phase_one(k, _):
        @pl.when(k < K)
        def _():
            own_to(k, 0, outer).wait_recv()
            fwd(k).start()
            pair_in(k).wait_recv()
            rel(k).start()
            own_to(k, 1, behind).wait_recv()
            own_to(k, 2, ahead).wait_recv()
            sib_a(k).start()

        @pl.when(k > 0)
        def _():
            sib_a_in(k - 1).wait_recv()
            pair_job(0, k - 1)

            @pl.when(k == K)
            def _():
                send_partial(0)

            acc_own[...] += pull(block[grp], col_own[...], ga[k - 1], e_row_of(e_a, k - 1, 3))

        return 0

    lax.fori_loop(0, K + 1, phase_one, 0)
    sib_pair.start()
    e_rel.wait_recv()
    e_out.start()

    def pass_on(k):
        rel(k).wait_recv()
        rel_out(k).start()

    def pair_tiles(t, _):
        pass_on(t - 1)

        def step(k, _):
            pair_job(t, k)
            return 0

        lax.fori_loop(0, K, step, 0)
        send_partial(t)
        return 0

    lax.fori_loop(1, TILES, pair_tiles, 0)
    for k in range(TILES - 1, 3):
        pass_on(k)

    sib_own_in.wait_recv()
    sib_pair_in.wait_recv()
    local = partner_ref[...] - blk * (4 * ROWS)
    local = columns_of(tile_of(local.astype(jnp.float32))).astype(jnp.int32)
    local = jnp.concatenate([local] * (ROWS // 128), axis=1)
    lanes = lax.broadcasted_iota(jnp.int32, (ROWS, ROWS), 1)

    def positive(g, _):
        chosen = jnp.where(local == lanes + g * ROWS, -2.0, 0.0).astype(jnp.bfloat16)
        acc_own[...] += jnp.dot(chosen, block[g], preferred_element_type=jnp.float32)
        return 0

    lax.fori_loop(0, 4, positive, 0)

    e_fwd.wait_recv()
    e_out.wait_recv()
    e_sibb.start()
    e_sibb_in.wait_recv()

    def phase_two(k, _):
        @pl.when(k < K)
        def _():
            fwd(k).wait_recv()
            rel_out(k).wait_recv()
            sib_b(k).start()

        @pl.when(k < K - 3)
        def _():
            pass_on(k + 3)

        @pl.when(k > 0)
        def _():
            sib_b_in(k - 1).wait_recv()
            acc_own[...] += pull(block[grp], col_own[...], gb[k - 1], e_row_of(e_b, k - 1, 2))

        return 0

    lax.fori_loop(0, K + 1, phase_two, 0)

    def finish(t, _):
        partial(t).wait_recv()
        at = tile(t)
        inv = invs[at, 0:1]
        normed = emb[at, :] * inv
        unit = INV_TEMP * (acc_own[at, :] + part_in[at, :].astype(jnp.float32))
        radial = jnp.sum(normed * unit, axis=1, keepdims=True)
        out_ref[at, :] = inv * (unit - normed * radial)
        return 0

    lax.fori_loop(0, TILES, finish, 0)

    def drain(k, _):
        own_pair(k).wait_send()
        own_to(k, 0, outer).wait_send()
        own_to(k, 1, behind).wait_send()
        own_to(k, 2, ahead).wait_send()
        sib_a(k).wait_send()
        fwd(k).wait_send()
        rel(k).wait_send()
        rel_out(k).wait_send()
        sib_b(k).wait_send()
        return 0

    lax.fori_loop(0, K, drain, 0)
    for t in range(TILES):
        partial(t).wait_send()
    for copy in e_copies + [e_sib, e_fwd, e_rel, e_out, e_sibb, sib_own, sib_pair]:
        copy.wait_send()


def solution(mesh):
    blocks = mesh.shape["blk"]
    bf16, f32 = jnp.bfloat16, jnp.float32
    dma = pltpu.SemaphoreType.DMA

    def per_device(embeddings, normalizers, partner_index):
        vmem = pl.BlockSpec(memory_space=pltpu.VMEM)
        return pl.pallas_call(
            functools.partial(kernel, blocks),
            out_shape=jax.ShapeDtypeStruct((ROWS, D), f32),
            in_specs=[pl.BlockSpec(memory_space=pl.ANY), vmem, vmem],
            out_specs=vmem,
            scratch_shapes=[
                pltpu.VMEM((ROWS, D), f32),
                pltpu.VMEM((ROWS, 128), f32),
                pltpu.VMEM((4, ROWS, D), bf16),
                pltpu.VMEM((K, 6 * R, D), bf16),
                pltpu.VMEM((K, 4 * R, D), bf16),
                pltpu.VMEM((K, R, D), bf16),
                pltpu.VMEM((ROWS, D), f32),
                pltpu.VMEM((ROWS, D), f32),
                pltpu.VMEM((ROWS, D), bf16),
                pltpu.VMEM((ROWS, D), bf16),
                pltpu.VMEM((8, 128), f32),
                pltpu.VMEM((8, 128), f32),
                pltpu.VMEM((2, 3, 8, 128), f32),
                pltpu.VMEM((8, 128), f32),
                pltpu.VMEM((2, 2, 8, 128), f32),
                pltpu.VMEM((ROWS, 128), f32),
                pltpu.VMEM((ROWS, 128), f32),
                dma, dma((2,)), dma((2,)), dma((4, K)), dma((4, K)), dma((K,)), dma((K,)),
                dma((K,)), dma((K,)), dma((K,)), dma((K,)), dma((K,)), dma((K,)), dma((K,)), dma((K,)),
                dma((TILES,)), dma((TILES,)), dma((9,)), dma((9,)),
            ],
            compiler_params=pltpu.CompilerParams(
                collective_id=0, has_side_effects=True, vmem_limit_bytes=48 << 20
            ),
            cost_estimate=pl.CostEstimate(
                flops=10 * 10**9, bytes_accessed=4 << 20, transcendentals=3 * 10**6
            ),
        )(embeddings, normalizers.reshape(1, ROWS), partner_index.reshape(1, ROWS))

    placed = (P(("blk", "grp"), None), P(("blk", "grp")), P(("blk", "grp")))
    return jax.shard_map(
        per_device, mesh=mesh, in_specs=placed, out_specs=P(("blk", "grp"), None), check_vma=False
    )
```

time: 321 us -> 66.2 us (0.21)
  the two profiles are of different devices: /device:TPU:28 before, /device:TPU:1 now
where the time goes in v1:
time: 66.2 us; the launch traced here: 66.1 us
  Pallas kernels  62.2 us (94%)
  local copies, waits for them, and re-layouts  3.92 us (6%)
    pallas_call x1, Pallas kernels, per_device(): pl.pallas_call(functools.partial(kernel, blocks), out_shape=jax.ShapeDtyp...  62.2 us
    unnamed x3, local copies, waits for them, and re-layouts  2.55 us

profile of v1, /device:TPU:1, one launch (start us, length us, event | category | flops | bytes accessed | tf_op | source)
XLA Modules:
  0.0 66.1 jit_solution(3442657029971213116)
XLA Ops:
  0.0 0.7 %reshape.6.norm_ref = bf16[1,384]{1,0:T(2,128)(2,1)S(1)} reshape(bf16[384]{0:T(512)(128)(2,1)} %param.4) | data formatting | bytes 1536 | tf_op jit(solution)/shard_map/reshape | solution.py:358
  0.7 0.7 %reshape.7.partner_ref = s32[1,384]{1,0:T(1,128)S(1)} reshape(s32[384]{0:T(512)} %param.5) | data formatting | bytes 3072 | tf_op jit(solution)/shard_map/reshape | solution.py:358
  1.4 0.0 copy-start
  1.4 1.4 %copy-done = f32[384,1024]{1,0:T(8,128)S(1)} copy-done((f32[384,1024]{1,0:T(8,128)S(1)}, f32[384,1024]{1,0:T(8,128)}, u32[]{:S(2)}) %copy-start) | copy-done | bytes 1572888
  2.8 62.2 %shard_map.37 = f32[384,1024]{1,0:T(8,128)S(1)} custom-call(f32[384,1024]{1,0:T(8,128)S(1)} %copy-done, bf16[1,384]{1,0:T(2,128)(2,1)S(1)} %reshape.6.norm_ref, s32[1,384]{1,0:T(1,128)S(1)} %reshape.7.partner_ref), custom_call_target="tpu_custom_call" | custom-call | flops 10000000000 | bytes 4194304 | tf_op jit(solution)/shard_map/pallas_call | solution.py:325
  65.0 1.1 %copy.5 = f32[384,1024]{1,0:T(8,128)} copy(f32[384,1024]{1,0:T(8,128)S(1)} %shard_map.37) | data formatting | bytes 3145728
Async XLA Ops:
  1.4 1.4 %copy-start = (f32[384,1024]{1,0:T(8,128)S(1)}, f32[384,1024]{1,0:T(8,128)}, u32[]{:S(2)}) copy-start(f32[384,1024]{1,0:T(8,128)} %emb_hbm.1) | copy-start | bytes 4718596

commit v2 on v0

v2 whole, which is shorter than its diff:
```python
import functools

import jax
import jax.numpy as jnp
from jax import lax
from jax.experimental import pallas as pl
from jax.experimental.pallas import tpu as pltpu
from jax.sharding import PartitionSpec as P

MESH = pl.DeviceIdType.MESH
ROWS = 384
D = 1024
K = 6
R = ROWS // K
N2 = 12
R2 = ROWS // N2
T = 128
TILES = ROWS // T
INV_TEMP = 10.0
SCALE = INV_TEMP * 1.4426950408889634


def tile_of(row):
    pieces = [row[:, k * R : (k + 1) * R] for k in range(K)]
    body = jnp.concatenate(pieces + [jnp.zeros((8 - K, R), row.dtype)], axis=0)
    return jnp.concatenate([body, jnp.zeros((8, 128 - R), row.dtype)], axis=1)


def columns_of(tile):
    turned = jnp.transpose(jnp.concatenate([tile] * 16, axis=0))
    return jnp.concatenate(
        [jnp.broadcast_to(turned[0:R, k : k + 1], (R, 128)) for k in range(K)], axis=0
    )


def kernel(
    blocks, emb_hbm, norm_hbm, partner_hbm, out_ref,
    emb, norm, partner, invs, work, others, ga, gb1, gb2, relay, acc, part_out, part_in,
    e_own, e_pair, e_a, e_relay, e_b, col, row_a, row_b1, row_b2,
    load_s, small_s, sib_s, sib_r, own_s, own_r, siba_s, siba_r, fwd_s, fwd_r, rel_s, rel_r,
    out_s, out_r, sib1_s, sib1_r, sib2_s, sib2_r, part_s, part_r, e_s, e_r,
):
    blk = lax.axis_index("blk")
    grp = lax.axis_index("grp")
    x_hi = blk % 2
    x_lo = grp // 2
    core = grp % 2
    turn = 2 * (1 - 2 * x_hi)
    pair_grp = (1 - x_lo) * 2 + core
    sib_grp = x_lo * 2 + 1 - core
    cross_grp = (1 - x_lo) * 2 + 1 - core
    sib = (blk, sib_grp)
    pair = (blk, pair_grp)
    outer = (blk + 1 - 2 * x_hi, pair_grp)
    ahead = ((blk + turn + blocks) % blocks, grp)
    behind = ((blk - turn + blocks) % blocks, grp)

    def remote(src, dst, send, recv, to):
        return pltpu.make_async_remote_copy(
            src_ref=src, dst_ref=dst, send_sem=send, recv_sem=recv, device_id=to, device_id_type=MESH
        )

    def rows(at, n):
        return pl.ds(at, n)

    def laned(at, c, n):
        return pl.ds(pl.multiple_of(at + c * n, 16), n)

    def lane_a(k, stream):
        return pl.ds(pl.multiple_of((k * 6 + stream + core * 3) * R, 16), R)

    loads = [
        pltpu.make_async_copy(emb_hbm.at[rows(k * R, R)], emb.at[rows(k * R, R)], load_s.at[k])
        for k in range(K)
    ]
    small = [
        pltpu.make_async_copy(norm_hbm, norm, small_s.at[0]),
        pltpu.make_async_copy(partner_hbm, partner, small_s.at[1]),
    ]
    small[0].start()
    for copy in loads:
        copy.start()
    small[1].start()
    barrier = pltpu.get_barrier_semaphore()
    neighbours = (sib, pair, outer, ahead, behind)
    for to in neighbours:
        pl.semaphore_signal(barrier, inc=1, device_id=to, device_id_type=MESH)

    small[0].wait()
    e_tile = tile_of(jnp.exp(-norm[...].astype(jnp.float32)).reshape(1, ROWS))
    e_own[...] = e_tile

    def normalize(k):
        loads[k].wait()
        at = rows(k * R, R)
        x = emb[at, :]
        inv = lax.rsqrt(jnp.sum(x * x, axis=1, keepdims=True) + 1e-06)
        invs[at, :] = jnp.broadcast_to(inv, (R, 128))
        work[at, :] = (x * inv).astype(jnp.bfloat16)

    e_copies = [
        remote(e_own, e_pair, e_s.at[0], e_r.at[0], pair),
        remote(e_own, e_a.at[core, 0], e_s.at[1], e_r.at[1], outer),
        remote(e_own, e_a.at[core, 1], e_s.at[2], e_r.at[2], behind),
        remote(e_own, e_a.at[core, 2], e_s.at[3], e_r.at[3], ahead),
    ]
    e_sib = remote(e_a.at[core], e_a.at[core], e_s.at[4], e_r.at[4], sib)
    e_sib_in = remote(e_a.at[1 - core], e_a.at[1 - core], e_s.at[4], e_r.at[4], sib)
    e_fwd = remote(e_a.at[core, 0], e_b.at[core, 0], e_s.at[5], e_r.at[5], ahead)
    e_rel = remote(e_pair, e_relay, e_s.at[6], e_r.at[6], behind)
    e_out = remote(e_relay, e_b.at[core, 1], e_s.at[7], e_r.at[7], outer)
    e_sibb = remote(e_b.at[core], e_b.at[core], e_s.at[8], e_r.at[8], sib)
    e_sibb_in = remote(e_b.at[1 - core], e_b.at[1 - core], e_s.at[8], e_r.at[8], sib)

    own_pair = [
        remote(work.at[rows(k * R, R)], work.at[rows(ROWS + k * R, R)], own_s.at[0, k], own_r.at[0, k], pair)
        for k in range(K)
    ]

    def own_to(stream, to):
        return [
            remote(
                work.at[rows(k * R, R)], ga.at[lane_a(k, stream)],
                own_s.at[1 + stream, k], own_r.at[1 + stream, k], to,
            )
            for k in range(K)
        ]

    own_outer, own_behind, own_ahead = own_to(0, outer), own_to(1, behind), own_to(2, ahead)

    def both_ways(ref, at, n, send, recv):
        mine = ref.at[laned(at, core, n)]
        theirs = ref.at[laned(at, 1 - core, n)]
        return remote(mine, mine, send, recv, sib), remote(theirs, theirs, send, recv, sib)

    sib_a = [both_ways(ga, k * 6 * R, 3 * R, siba_s.at[k], siba_r.at[k]) for k in range(K)]
    sib_1 = [both_ways(gb1, k * 2 * R, R, sib1_s.at[k], sib1_r.at[k]) for k in range(K)]
    sib_2 = [both_ways(gb2, i * 2 * R2, R2, sib2_s.at[i], sib2_r.at[i]) for i in range(N2)]
    fwd = [
        remote(
            ga.at[lane_a(k, 0)],
            gb1.at[laned(k * 2 * R, core, R)], fwd_s.at[k], fwd_r.at[k], ahead,
        )
        for k in range(K)
    ]
    rel = [
        remote(work.at[rows(ROWS + i * R2, R2)], relay.at[rows(i * R2, R2)], rel_s.at[i], rel_r.at[i], behind)
        for i in range(N2)
    ]
    rel_out = [
        remote(relay.at[rows(i * R2, R2)], gb2.at[laned(i * 2 * R2, core, R2)], out_s.at[i], out_r.at[i], outer)
        for i in range(N2)
    ]
    partial = [
        remote(part_out.at[rows(t * T, T)], part_in.at[rows(t * T, T)], part_s.at[t], part_r.at[t], pair)
        for t in range(TILES)
    ]
    sib_own = remote(work.at[rows(0, ROWS)], others.at[0], sib_s.at[0], sib_r.at[0], sib)
    sib_pair = remote(work.at[rows(ROWS, ROWS)], others.at[1], sib_s.at[1], sib_r.at[1], sib)

    normalize(0)
    pl.semaphore_wait(barrier, len(neighbours))
    for copy in e_copies:
        copy.start()
    for k in range(K):
        own_pair[k].start()
        own_outer[k].start()
        own_behind[k].start()
        own_ahead[k].start()
        if k + 1 < K:
            normalize(k + 1)
    sib_own.start()
    col[0:ROWS, :] = columns_of(e_tile)

    for copy in e_copies:
        copy.wait_recv()
    e_sib.start()
    e_fwd.start()
    e_rel.start()
    col[ROWS : 2 * ROWS, :] = columns_of(e_pair[...])
    e_sib_in.wait_recv()
    row_a[0:1, :] = jnp.concatenate(
        [e_a[c, s, k : k + 1, 0:R] for k in range(K) for c in range(2) for s in range(3)], axis=1
    )

    def pull(r0, m, guests, row, g0, g, first=False):
        own, met = rows(r0, m), guests[rows(g0, g), :]
        scores = lax.dot_general(
            work[own, :], met, (((1,), (1,)), ((), ())), preferred_element_type=jnp.float32
        )
        spread = jnp.concatenate([col[own, :]] * (g // 128), axis=1) + row[0:1, g0 : g0 + g]
        weights = (jnp.exp2(scores * SCALE) * spread).astype(jnp.bfloat16)
        add = jnp.dot(weights, met, preferred_element_type=jnp.float32)
        acc[own, :] = add if first else acc[own, :] + add

    def pull_a(r0, m, k, n, first=False):
        pull(r0, m, ga, row_a, k * 6 * R, n * 6 * R, first)

    p0, p1, p2 = ROWS, ROWS + T, ROWS + 2 * T

    def arrive(k):
        own_outer[k].wait_recv()
        fwd[k].start()
        own_pair[k].wait_recv()
        rel[2 * k].start()
        rel[2 * k + 1].start()
        own_behind[k].wait_recv()
        own_ahead[k].wait_recv()
        sib_a[k][0].start()

    def send_partial(t):
        part_out[rows(t * T, T), :] = acc[rows(ROWS + t * T, T), :].astype(jnp.bfloat16)
        partial[t].start()

    def pass_on(i):
        rel[i].wait_recv()
        rel_out[i].start()

    small[1].wait()
    local = partner[...].reshape(1, ROWS) - blk * (4 * ROWS)
    local = columns_of(tile_of(local.astype(jnp.float32))).astype(jnp.int32)

    def positive(held, g):
        lanes = lax.broadcasted_iota(jnp.int32, (ROWS, ROWS), 1) + g * ROWS
        spread = jnp.concatenate([local] * (ROWS // 128), axis=1)
        chosen = jnp.where(spread == lanes, -2.0, 0.0).astype(jnp.bfloat16)
        acc[0:ROWS, :] += jnp.dot(chosen, held[...], preferred_element_type=jnp.float32)

    arrive(0)
    arrive(1)
    sib_a[0][1].wait_recv()
    sib_a[1][1].wait_recv()
    pull_a(0, ROWS + T, 0, 2, first=True)
    arrive(2)
    sib_own.wait_recv()
    positive(work.at[rows(0, ROWS)], grp)
    positive(others.at[0], sib_grp)
    arrive(3)
    pull_a(p1, T, 0, 2, first=True)
    sib_a[2][1].wait_recv()
    sib_a[3][1].wait_recv()
    pull_a(0, ROWS + T, 2, 2)
    arrive(4)
    pull_a(p1, T, 2, 2)
    arrive(5)
    sib_a[4][1].wait_recv()
    pull_a(p0, T, 4, 1)
    pull_a(p2, T, 0, 2, first=True)
    e_rel.wait_recv()
    e_out.start()
    pass_on(0)
    sib_a[5][1].wait_recv()
    pull_a(p0, T, 5, 1)
    send_partial(0)
    sib_pair.start()
    pass_on(1)
    pull_a(p1, T, 4, 2)
    send_partial(1)
    pass_on(2)
    pull_a(p2, T, 2, 2)
    pass_on(3)
    pull_a(p2, T, 4, 2)
    send_partial(2)
    pass_on(4)
    pull_a(0, ROWS, 4, 1)
    pass_on(5)
    pull_a(0, ROWS, 5, 1)
    pass_on(6)
    sib_pair.wait_recv()
    positive(work.at[rows(ROWS, ROWS)], pair_grp)
    positive(others.at[1], cross_grp)
    pass_on(7)

    def arrive_1(k):
        fwd[k].wait_recv()
        sib_1[k][0].start()

    def arrive_2(i):
        rel_out[i].wait_recv()
        sib_2[i][0].start()

    e_fwd.wait_recv()
    e_out.wait_recv()
    e_sibb.start()
    for k in range(3):
        arrive_1(k)
    for i in range(4):
        arrive_2(i)
    pass_on(8)
    e_sibb_in.wait_recv()
    row_b1[0:1, :] = jnp.concatenate(
        [e_b[c, 0, k : k + 1, 0:R] for k in range(K) for c in range(2)], axis=1
    )
    row_b2[0:1, :] = jnp.concatenate(
        [
            e_b[c, 1, i // 2 : i // 2 + 1, (i % 2) * R2 : (i % 2 + 1) * R2]
            for i in range(N2)
            for c in range(2)
        ],
        axis=1,
    )
    arrive_1(3)
    arrive_2(4)
    arrive_2(5)
    pass_on(9)
    arrive_1(4)
    pass_on(10)
    for k in range(4):
        sib_1[k][1].wait_recv()
    pull(0, ROWS, gb1, row_b1, 0, 8 * R)
    pass_on(11)
    arrive_2(6)
    arrive_2(7)
    arrive_1(5)
    for i in range(6):
        sib_2[i][1].wait_recv()
    pull(0, ROWS, gb2, row_b2, 0, 12 * R2)
    arrive_2(8)
    arrive_2(9)
    for k in range(4, 6):
        sib_1[k][1].wait_recv()
    pull(0, ROWS, gb1, row_b1, 8 * R, 4 * R)
    arrive_2(10)
    arrive_2(11)
    for i in range(6, 10):
        sib_2[i][1].wait_recv()
    pull(0, ROWS, gb2, row_b2, 12 * R2, 8 * R2)
    for i in range(10, 12):
        sib_2[i][1].wait_recv()
    pull(0, ROWS, gb2, row_b2, 20 * R2, 4 * R2)

    for t in range(TILES):
        partial[t].wait_recv()
        at = rows(t * T, T)
        inv = invs[at, 0:1]
        normed = emb[at, :] * inv
        unit = INV_TEMP * (acc[at, :] + part_in[at, :].astype(jnp.float32))
        radial = jnp.sum(normed * unit, axis=1, keepdims=True)
        out_ref[at, :] = inv * (unit - normed * radial)

    for copies in (own_pair, own_outer, own_behind, own_ahead, fwd, rel, rel_out, partial, e_copies):
        for copy in copies:
            copy.wait_send()
    for copies in (sib_a, sib_1, sib_2):
        for copy, _ in copies:
            copy.wait_send()
    for copy in (e_sib, e_fwd, e_rel, e_out, e_sibb, sib_own, sib_pair):
        copy.wait_send()


def solution(mesh):
    blocks = mesh.shape["blk"]
    bf16, f32 = jnp.bfloat16, jnp.float32
    dma = pltpu.SemaphoreType.DMA

    def per_device(embeddings, normalizers, partner_index):
        return pl.pallas_call(
            functools.partial(kernel, blocks),
            out_shape=jax.ShapeDtypeStruct((ROWS, D), f32),
            in_specs=[pl.BlockSpec(memory_space=pltpu.HBM)] * 3,
            out_specs=pl.BlockSpec(memory_space=pltpu.VMEM),
            scratch_shapes=[
                pltpu.VMEM((ROWS, D), f32),
                pltpu.VMEM((ROWS,), bf16),
                pltpu.VMEM((ROWS,), jnp.int32),
                pltpu.VMEM((ROWS, 128), f32),
                pltpu.VMEM((2 * ROWS, D), bf16),
                pltpu.VMEM((2, ROWS, D), bf16),
                pltpu.VMEM((6 * ROWS, D), bf16),
                pltpu.VMEM((2 * ROWS, D), bf16),
                pltpu.VMEM((2 * ROWS, D), bf16),
                pltpu.VMEM((ROWS, D), bf16),
                pltpu.VMEM((2 * ROWS, D), f32),
                pltpu.VMEM((ROWS, D), bf16),
                pltpu.VMEM((ROWS, D), bf16),
                pltpu.VMEM((8, 128), f32),
                pltpu.VMEM((8, 128), f32),
                pltpu.VMEM((2, 3, 8, 128), f32),
                pltpu.VMEM((8, 128), f32),
                pltpu.VMEM((2, 2, 8, 128), f32),
                pltpu.VMEM((2 * ROWS, 128), f32),
                pltpu.VMEM((8, 6 * ROWS), f32),
                pltpu.VMEM((8, 2 * ROWS), f32),
                pltpu.VMEM((8, 2 * ROWS), f32),
                dma((K,)), dma((2,)), dma((2,)), dma((2,)), dma((4, K)), dma((4, K)),
                dma((K,)), dma((K,)), dma((K,)), dma((K,)), dma((N2,)), dma((N2,)),
                dma((N2,)), dma((N2,)), dma((K,)), dma((K,)), dma((N2,)), dma((N2,)),
                dma((TILES,)), dma((TILES,)), dma((9,)), dma((9,)),
            ],
            compiler_params=pltpu.CompilerParams(
                collective_id=0, has_side_effects=True, vmem_limit_bytes=48 << 20
            ),
            cost_estimate=pl.CostEstimate(
                flops=10 * 10**9, bytes_accessed=4 << 20, transcendentals=3 * 10**6
            ),
        )(*[pltpu.with_memory_space_constraint(a, pltpu.HBM) for a in (embeddings, normalizers, partner_index)])

    placed = (P(("blk", "grp"), None), P(("blk", "grp")), P(("blk", "grp")))
    return jax.shard_map(
        per_device, mesh=mesh, in_specs=placed, out_specs=P(("blk", "grp"), None), check_vma=False
    )
```

time: 321 us -> 56.9 us (0.18)
  the two profiles are of different devices: /device:TPU:28 before, /device:TPU:1 now
where the time goes in v2:
time: 56.9 us; the launch traced here: 56.8 us
  Pallas kernels  55.7 us (98%)
  local copies, waits for them, and re-layouts  1.15 us (2%)
    pallas_call x1, Pallas kernels, per_device(): pl.pallas_call(functools.partial(kernel, blocks), out_shape=jax.ShapeDtyp...  55.7 us
    unnamed x1, local copies, waits for them, and re-layouts  1.15 us

profile of v2, /device:TPU:1, one launch (start us, length us, event | category | flops | bytes accessed | tf_op | source)
XLA Modules:
  0.0 56.8 jit_solution(15111013213805833505)
XLA Ops:
  0.0 55.7 %shard_map.37 = f32[384,1024]{1,0:T(8,128)S(1)} custom-call(f32[384,1024]{1,0:T(8,128)} %emb_hbm.1, bf16[384]{0:T(512)(128)(2,1)} %norm_hbm.1, s32[384]{0:T(512)} %partner_hbm.1), custom_call_target="tpu_custom_call" | custom-call | flops 10000000000 | bytes 4194304 | tf_op jit(solution)/shard_map/pallas_call | solution.py:357
  55.7 1.1 %copy.5 = f32[384,1024]{1,0:T(8,128)} copy(f32[384,1024]{1,0:T(8,128)S(1)} %shard_map.37) | data formatting | bytes 3145728

commit v3 on v2

--- a/solution.py
+++ b/solution.py
@@ -14,6 +14,7 @@
 R = ROWS // K
 N2 = 12
 R2 = ROWS // N2
+NP = 3
 T = 128
 TILES = ROWS // T
 INV_TEMP = 10.0
@@ -35,8 +36,8 @@
 
 def kernel(
     blocks, emb_hbm, norm_hbm, partner_hbm, out_ref,
-    emb, norm, partner, invs, work, others, ga, gb1, gb2, relay, acc, part_out, part_in,
-    e_own, e_pair, e_a, e_relay, e_b, col, row_a, row_b1, row_b2,
+    emb, norm, partner, invs, work, others, ga, gb, relay, acc, part_out, part_in,
+    e_own, e_pair, e_a, e_relay, e_b, col, row_a, row_b,
     load_s, small_s, sib_s, sib_r, own_s, own_r, siba_s, siba_r, fwd_s, fwd_r, rel_s, rel_r,
     out_s, out_r, sib1_s, sib1_r, sib2_s, sib2_r, part_s, part_r, e_s, e_r,
 ):
@@ -134,21 +135,30 @@
         return remote(mine, mine, send, recv, sib), remote(theirs, theirs, send, recv, sib)
 
     sib_a = [both_ways(ga, k * 6 * R, 3 * R, siba_s.at[k], siba_r.at[k]) for k in range(K)]
-    sib_1 = [both_ways(gb1, k * 2 * R, R, sib1_s.at[k], sib1_r.at[k]) for k in range(K)]
-    sib_2 = [both_ways(gb2, i * 2 * R2, R2, sib2_s.at[i], sib2_r.at[i]) for i in range(N2)]
+    at_1 = [k * 2 * R + (0 if k < 4 else 8 * R) for k in range(K)]
+    at_2 = [i * 2 * R2 + (8 * R if i < 8 else 12 * R) for i in range(N2)]
+    sib_1 = [both_ways(gb, at_1[k], R, sib1_s.at[k], sib1_r.at[k]) for k in range(K)]
+    sib_2 = [both_ways(gb, at_2[i], R2, sib2_s.at[i], sib2_r.at[i]) for i in range(N2)]
     fwd = [
         remote(
             ga.at[lane_a(k, 0)],
-            gb1.at[laned(k * 2 * R, core, R)], fwd_s.at[k], fwd_r.at[k], ahead,
+            gb.at[laned(at_1[k], core, R)], fwd_s.at[k], fwd_r.at[k], ahead,
         )
         for k in range(K)
     ]
+
+    def lane_rel(i):
+        return pl.ds(pl.multiple_of((i // 2 * 6 + 1 + core * 3) * R + i % 2 * R2, 16), R2)
+
     rel = [
-        remote(work.at[rows(ROWS + i * R2, R2)], relay.at[rows(i * R2, R2)], rel_s.at[i], rel_r.at[i], behind)
+        remote(
+            ga.at[lane_rel(i)] if i < NP else work.at[rows(ROWS + i * R2, R2)],
+            relay.at[rows(i * R2, R2)], rel_s.at[i], rel_r.at[i], pair if i < NP else behind,
+        )
         for i in range(N2)
     ]
     rel_out = [
-        remote(relay.at[rows(i * R2, R2)], gb2.at[laned(i * 2 * R2, core, R2)], out_s.at[i], out_r.at[i], outer)
+        remote(relay.at[rows(i * R2, R2)], gb.at[laned(at_2[i], core, R2)], out_s.at[i], out_r.at[i], outer)
         for i in range(N2)
     ]
     partial = [
@@ -163,7 +173,8 @@
     for copy in e_copies:
         copy.start()
     for k in range(K):
-        own_pair[k].start()
+        if k < 4:
+            own_pair[k].start()
         own_outer[k].start()
         own_behind[k].start()
         own_ahead[k].start()
@@ -171,6 +182,20 @@
             normalize(k + 1)
     sib_own.start()
     col[0:ROWS, :] = columns_of(e_tile)
+
+    small[1].wait()
+    local = partner[...].reshape(1, ROWS) - blk * (4 * ROWS)
+    local = columns_of(tile_of(local.astype(jnp.float32))).astype(jnp.int32)
+
+    def positive(held, g, first=False):
+        lanes = lax.broadcasted_iota(jnp.int32, (ROWS, ROWS), 1) + g * ROWS
+        spread = jnp.concatenate([local] * (ROWS // 128), axis=1)
+        chosen = jnp.where(spread == lanes, -2.0, 0.0).astype(jnp.bfloat16)
+        add = jnp.dot(chosen, held[...], preferred_element_type=jnp.float32)
+        acc[0:ROWS, :] = add if first else acc[0:ROWS, :] + add
+
+    positive(work.at[rows(0, ROWS)], grp, first=True)
+    acc[ROWS : ROWS + T, :] = jnp.zeros((T, D), jnp.float32)
 
     for copy in e_copies:
         copy.wait_recv()
@@ -201,12 +226,23 @@
     def arrive(k):
         own_outer[k].wait_recv()
         fwd[k].start()
-        own_pair[k].wait_recv()
-        rel[2 * k].start()
-        rel[2 * k + 1].start()
         own_behind[k].wait_recv()
+        for i in (2 * k, 2 * k + 1):
+            if i < NP:
+                rel[i].start()
+        if k == 1:
+            own_pair[4].start()
+            own_pair[5].start()
         own_ahead[k].wait_recv()
         sib_a[k][0].start()
+        if k < 4:
+            arrive_pair(k)
+
+    def arrive_pair(k):
+        own_pair[k].wait_recv()
+        for i in (2 * k, 2 * k + 1):
+            if i >= NP:
+                rel[i].start()
 
     def send_partial(t):
         part_out[rows(t * T, T), :] = acc[rows(ROWS + t * T, T), :].astype(jnp.bfloat16)
@@ -216,60 +252,52 @@
         rel[i].wait_recv()
         rel_out[i].start()
 
-    small[1].wait()
-    local = partner[...].reshape(1, ROWS) - blk * (4 * ROWS)
-    local = columns_of(tile_of(local.astype(jnp.float32))).astype(jnp.int32)
-
-    def positive(held, g):
-        lanes = lax.broadcasted_iota(jnp.int32, (ROWS, ROWS), 1) + g * ROWS
-        spread = jnp.concatenate([local] * (ROWS // 128), axis=1)
-        chosen = jnp.where(spread == lanes, -2.0, 0.0).astype(jnp.bfloat16)
-        acc[0:ROWS, :] += jnp.dot(chosen, held[...], preferred_element_type=jnp.float32)
-
     arrive(0)
+    sib_own.wait_recv()
+    positive(others.at[0], sib_grp)
     arrive(1)
     sib_a[0][1].wait_recv()
     sib_a[1][1].wait_recv()
-    pull_a(0, ROWS + T, 0, 2, first=True)
+    pull_a(0, ROWS + T, 0, 2)
     arrive(2)
-    sib_own.wait_recv()
-    positive(work.at[rows(0, ROWS)], grp)
-    positive(others.at[0], sib_grp)
     arrive(3)
     pull_a(p1, T, 0, 2, first=True)
+    pass_on(0)
     sib_a[2][1].wait_recv()
     sib_a[3][1].wait_recv()
-    pull_a(0, ROWS + T, 2, 2)
+    pass_on(1)
     arrive(4)
-    pull_a(p1, T, 2, 2)
+    pull_a(0, ROWS + 2 * T, 2, 2)
     arrive(5)
+    pass_on(2)
+    pass_on(3)
     sib_a[4][1].wait_recv()
-    pull_a(p0, T, 4, 1)
-    pull_a(p2, T, 0, 2, first=True)
+    pull_a(p0, 2 * T, 4, 1)
+    pass_on(4)
+    sib_a[5][1].wait_recv()
+    pull_a(p0, 2 * T, 5, 1)
+    send_partial(0)
+    send_partial(1)
+    pass_on(5)
     e_rel.wait_recv()
     e_out.start()
-    pass_on(0)
-    sib_a[5][1].wait_recv()
-    pull_a(p0, T, 5, 1)
-    send_partial(0)
+    arrive_pair(4)
+    pass_on(6)
+    pull_a(0, ROWS, 4, 2)
+    pass_on(7)
+    arrive_pair(5)
     sib_pair.start()
-    pass_on(1)
-    pull_a(p1, T, 4, 2)
-    send_partial(1)
-    pass_on(2)
+    pull_a(p2, T, 0, 2, first=True)
+    pass_on(8)
     pull_a(p2, T, 2, 2)
-    pass_on(3)
+    pass_on(9)
     pull_a(p2, T, 4, 2)
     send_partial(2)
-    pass_on(4)
-    pull_a(0, ROWS, 4, 1)
-    pass_on(5)
-    pull_a(0, ROWS, 5, 1)
-    pass_on(6)
+    pass_on(10)
     sib_pair.wait_recv()
     positive(work.at[rows(ROWS, ROWS)], pair_grp)
     positive(others.at[1], cross_grp)
-    pass_on(7)
+    pass_on(11)
 
     def arrive_1(k):
         fwd[k].wait_recv()
@@ -282,52 +310,34 @@
     e_fwd.wait_recv()
     e_out.wait_recv()
     e_sibb.start()
-    for k in range(3):
+    for k in range(4):
         arrive_1(k)
-    for i in range(4):
+    for i in range(8):
         arrive_2(i)
-    pass_on(8)
     e_sibb_in.wait_recv()
-    row_b1[0:1, :] = jnp.concatenate(
-        [e_b[c, 0, k : k + 1, 0:R] for k in range(K) for c in range(2)], axis=1
-    )
-    row_b2[0:1, :] = jnp.concatenate(
-        [
-            e_b[c, 1, i // 2 : i // 2 + 1, (i % 2) * R2 : (i % 2 + 1) * R2]
-            for i in range(N2)
-            for c in range(2)
-        ],
-        axis=1,
-    )
-    arrive_1(3)
-    arrive_2(4)
-    arrive_2(5)
-    pass_on(9)
-    arrive_1(4)
-    pass_on(10)
+    first = [e_b[c, 0, k : k + 1, 0:R] for k in range(K) for c in range(2)]
+    second = [
+        e_b[c, 1, i // 2 : i // 2 + 1, (i % 2) * R2 : (i % 2 + 1) * R2] for i in range(N2) for c in range(2)
+    ]
+    row_b[0:1, :] = jnp.concatenate(first[:8] + second[:16] + first[8:] + second[16:], axis=1)
+
     for k in range(4):
         sib_1[k][1].wait_recv()
-    pull(0, ROWS, gb1, row_b1, 0, 8 * R)
-    pass_on(11)
-    arrive_2(6)
-    arrive_2(7)
-    arrive_1(5)
-    for i in range(6):
-        sib_2[i][1].wait_recv()
-    pull(0, ROWS, gb2, row_b2, 0, 12 * R2)
+    pull(0, ROWS, gb, row_b, 0, 8 * R)
     arrive_2(8)
     arrive_2(9)
-    for k in range(4, 6):
-        sib_1[k][1].wait_recv()
-    pull(0, ROWS, gb1, row_b1, 8 * R, 4 * R)
+    arrive_1(4)
+    for i in range(8):
+        sib_2[i][1].wait_recv()
+    pull(0, ROWS, gb, row_b, 8 * R, 8 * R)
     arrive_2(10)
     arrive_2(11)
-    for i in range(6, 10):
+    arrive_1(5)
+    for k in range(4, K):
+        sib_1[k][1].wait_recv()
+    for i in range(8, N2):
         sib_2[i][1].wait_recv()
-    pull(0, ROWS, gb2, row_b2, 12 * R2, 8 * R2)
-    for i in range(10, 12):
-        sib_2[i][1].wait_recv()
-    pull(0, ROWS, gb2, row_b2, 20 * R2, 4 * R2)
+    pull(0, ROWS, gb, row_b, 16 * R, 8 * R)
 
     for t in range(TILES):
         partial[t].wait_recv()
@@ -367,8 +377,7 @@
                 pltpu.VMEM((2 * ROWS, D), bf16),
                 pltpu.VMEM((2, ROWS, D), bf16),
                 pltpu.VMEM((6 * ROWS, D), bf16),
-                pltpu.VMEM((2 * ROWS, D), bf16),
-                pltpu.VMEM((2 * ROWS, D), bf16),
+                pltpu.VMEM((4 * ROWS, D), bf16),
                 pltpu.VMEM((ROWS, D), bf16),
                 pltpu.VMEM((2 * ROWS, D), f32),
                 pltpu.VMEM((ROWS, D), bf16),
@@ -380,8 +389,7 @@
                 pltpu.VMEM((2, 2, 8, 128), f32),
                 pltpu.VMEM((2 * ROWS, 128), f32),
                 pltpu.VMEM((8, 6 * ROWS), f32),
-                pltpu.VMEM((8, 2 * ROWS), f32),
-                pltpu.VMEM((8, 2 * ROWS), f32),
+                pltpu.VMEM((8, 4 * ROWS), f32),
                 dma((K,)), dma((2,)), dma((2,)), dma((2,)), dma((4, K)), dma((4, K)),
                 dma((K,)), dma((K,)), dma((K,)), dma((K,)), dma((N2,)), dma((N2,)),
                 dma((N2,)), dma((N2,)), dma((K,)), dma((K,)), dma((N2,)), dma((N2,)),

time: 56.9 us -> 55 us (0.967)
  Pallas kernels: 55.7 us -> 53.7 us
    pallas_call x1, Pallas kernels: 55.7 us -> 53.7 us  [per_device(): pl.pallas_call(functools.partial(kernel, blocks), out_shape=jax.ShapeDtyp...]
where the time goes in v3:
time: 55 us; the launch traced here: 54.9 us
  Pallas kernels  53.7 us (98%)
  local copies, waits for them, and re-layouts  1.15 us (2%)
    pallas_call x1, Pallas kernels, per_device(): pl.pallas_call(functools.partial(kernel, blocks), out_shape=jax.ShapeDtyp...  53.7 us
    unnamed x1, local copies, waits for them, and re-layouts  1.15 us

profile of v3, /device:TPU:1, one launch (start us, length us, event | category | flops | bytes accessed | tf_op | source)
XLA Modules:
  0.0 54.9 jit_solution(15713567446807832142)
XLA Ops:
  0.0 53.7 %shard_map.37 = f32[384,1024]{1,0:T(8,128)S(1)} custom-call(f32[384,1024]{1,0:T(8,128)} %emb_hbm.1, bf16[384]{0:T(512)(128)(2,1)} %norm_hbm.1, s32[384]{0:T(512)} %partner_hbm.1), custom_call_target="tpu_custom_call" | custom-call | flops 10000000000 | bytes 4194304 | tf_op jit(solution)/shard_map/pallas_call | solution.py:367
  53.7 1.1 %copy.5 = f32[384,1024]{1,0:T(8,128)} copy(f32[384,1024]{1,0:T(8,128)S(1)} %shard_map.37) | data formatting | bytes 3145728

commit v4 on v3

--- a/solution.py
+++ b/solution.py
@@ -16,7 +16,7 @@
 R2 = ROWS // N2
 NP = 3
 T = 128
-TILES = ROWS // T
+TILES = ((0, T), (T, T), (2 * T, T // 2), (2 * T + T // 2, T // 2))
 INV_TEMP = 10.0
 SCALE = INV_TEMP * 1.4426950408889634
 
@@ -162,8 +162,8 @@
         for i in range(N2)
     ]
     partial = [
-        remote(part_out.at[rows(t * T, T)], part_in.at[rows(t * T, T)], part_s.at[t], part_r.at[t], pair)
-        for t in range(TILES)
+        remote(part_out.at[rows(*at)], part_in.at[rows(*at)], part_s.at[t], part_r.at[t], pair)
+        for t, at in enumerate(TILES)
     ]
     sib_own = remote(work.at[rows(0, ROWS)], others.at[0], sib_s.at[0], sib_r.at[0], sib)
     sib_pair = remote(work.at[rows(ROWS, ROWS)], others.at[1], sib_s.at[1], sib_r.at[1], sib)
@@ -208,15 +208,23 @@
         [e_a[c, s, k : k + 1, 0:R] for k in range(K) for c in range(2) for s in range(3)], axis=1
     )
 
-    def pull(r0, m, guests, row, g0, g, first=False):
-        own, met = rows(r0, m), guests[rows(g0, g), :]
+    def pull_rows(r0, m, met, row, first=False):
+        own, g = rows(r0, m), met.shape[0]
         scores = lax.dot_general(
             work[own, :], met, (((1,), (1,)), ((), ())), preferred_element_type=jnp.float32
         )
-        spread = jnp.concatenate([col[own, :]] * (g // 128), axis=1) + row[0:1, g0 : g0 + g]
+        wide = [col[own, :]] * (g // 128) + ([col[own, 0 : g % 128]] if g % 128 else [])
+        spread = jnp.concatenate(wide, axis=1) + row
         weights = (jnp.exp2(scores * SCALE) * spread).astype(jnp.bfloat16)
         add = jnp.dot(weights, met, preferred_element_type=jnp.float32)
         acc[own, :] = add if first else acc[own, :] + add
+
+    def pull(r0, m, guests, row, g0, g, first=False):
+        pull_rows(r0, m, guests[rows(g0, g), :], row[0:1, g0 : g0 + g], first)
+
+    def pull_last(r0, m, c):
+        row = jnp.concatenate([e_a[c, s, K - 1 : K, 0:R] for s in range(3)], axis=1)
+        pull_rows(r0, m, ga[laned((K - 1) * 6 * R, c, 3 * R), :], row)
 
     def pull_a(r0, m, k, n, first=False):
         pull(r0, m, ga, row_a, k * 6 * R, n * 6 * R, first)
@@ -245,7 +253,8 @@
                 rel[i].start()
 
     def send_partial(t):
-        part_out[rows(t * T, T), :] = acc[rows(ROWS + t * T, T), :].astype(jnp.bfloat16)
+        at, n = TILES[t]
+        part_out[rows(at, n), :] = acc[rows(ROWS + at, n), :].astype(jnp.bfloat16)
         partial[t].start()
 
     def pass_on(i):
@@ -267,15 +276,17 @@
     sib_a[3][1].wait_recv()
     pass_on(1)
     arrive(4)
-    pull_a(0, ROWS + 2 * T, 2, 2)
+    pull_a(p0, 2 * T, 2, 2)
+    pass_on(2)
+    pull_a(0, ROWS, 2, 1)
     arrive(5)
-    pass_on(2)
     pass_on(3)
     sib_a[4][1].wait_recv()
     pull_a(p0, 2 * T, 4, 1)
+    pull_last(p0, 2 * T, core)
     pass_on(4)
     sib_a[5][1].wait_recv()
-    pull_a(p0, 2 * T, 5, 1)
+    pull_last(p0, 2 * T, 1 - core)
     send_partial(0)
     send_partial(1)
     pass_on(5)
@@ -283,7 +294,7 @@
     e_out.start()
     arrive_pair(4)
     pass_on(6)
-    pull_a(0, ROWS, 4, 2)
+    pull_a(0, ROWS, 3, 3)
     pass_on(7)
     arrive_pair(5)
     sib_pair.start()
@@ -293,6 +304,7 @@
     pass_on(9)
     pull_a(p2, T, 4, 2)
     send_partial(2)
+    send_partial(3)
     pass_on(10)
     sib_pair.wait_recv()
     positive(work.at[rows(ROWS, ROWS)], pair_grp)
@@ -339,22 +351,28 @@
         sib_2[i][1].wait_recv()
     pull(0, ROWS, gb, row_b, 16 * R, 8 * R)
 
-    for t in range(TILES):
+    def finish(t):
         partial[t].wait_recv()
-        at = rows(t * T, T)
+        at = rows(*TILES[t])
         inv = invs[at, 0:1]
         normed = emb[at, :] * inv
         unit = INV_TEMP * (acc[at, :] + part_in[at, :].astype(jnp.float32))
         radial = jnp.sum(normed * unit, axis=1, keepdims=True)
         out_ref[at, :] = inv * (unit - normed * radial)
 
-    for copies in (own_pair, own_outer, own_behind, own_ahead, fwd, rel, rel_out, partial, e_copies):
+    finish(0)
+    finish(1)
+    for copies in (own_pair, own_outer, own_behind, own_ahead, fwd, rel, rel_out, partial[:2], e_copies):
         for copy in copies:
             copy.wait_send()
     for copies in (sib_a, sib_1, sib_2):
         for copy, _ in copies:
             copy.wait_send()
     for copy in (e_sib, e_fwd, e_rel, e_out, e_sibb, sib_own, sib_pair):
+        copy.wait_send()
+    finish(2)
+    finish(3)
+    for copy in partial[2:]:
         copy.wait_send()
 
 
@@ -393,7 +411,7 @@
                 dma((K,)), dma((2,)), dma((2,)), dma((2,)), dma((4, K)), dma((4, K)),
                 dma((K,)), dma((K,)), dma((K,)), dma((K,)), dma((N2,)), dma((N2,)),
                 dma((N2,)), dma((N2,)), dma((K,)), dma((K,)), dma((N2,)), dma((N2,)),
-                dma((TILES,)), dma((TILES,)), dma((9,)), dma((9,)),
+                dma((len(TILES),)), dma((len(TILES),)), dma((9,)), dma((9,)),
             ],
             compiler_params=pltpu.CompilerParams(
                 collective_id=0, has_side_effects=True, vmem_limit_bytes=48 << 20

time: 55 us -> 54.1 us (0.984)
  Pallas kernels: 53.7 us -> 52.9 us
    pallas_call x1, Pallas kernels: 53.7 us -> 52.9 us  [per_device(): pl.pallas_call(functools.partial(kernel, blocks), out_shape=jax.ShapeDtyp...]
where the time goes in v4:
time: 54.1 us; the launch traced here: 54 us
  Pallas kernels  52.9 us (98%)
  local copies, waits for them, and re-layouts  1.15 us (2%)
    pallas_call x1, Pallas kernels, per_device(): pl.pallas_call(functools.partial(kernel, blocks), out_shape=jax.ShapeDtyp...  52.9 us
    unnamed x1, local copies, waits for them, and re-layouts  1.15 us

profile of v4, /device:TPU:1, one launch (start us, length us, event | category | flops | bytes accessed | tf_op | source)
XLA Modules:
  0.0 54.0 jit_solution(9742212384755782669)
XLA Ops:
  0.0 52.9 %shard_map.37 = f32[384,1024]{1,0:T(8,128)S(1)} custom-call(f32[384,1024]{1,0:T(8,128)} %emb_hbm.1, bf16[384]{0:T(512)(128)(2,1)} %norm_hbm.1, s32[384]{0:T(512)} %partner_hbm.1), custom_call_target="tpu_custom_call" | custom-call | flops 10000000000 | bytes 4194304 | tf_op jit(solution)/shard_map/pallas_call | solution.py:385
  52.9 1.1 %copy.5 = f32[384,1024]{1,0:T(8,128)} copy(f32[384,1024]{1,0:T(8,128)S(1)} %shard_map.37) | data formatting | bytes 3145728

commit v5 on v4

--- a/solution.py
+++ b/solution.py
@@ -134,7 +134,16 @@
         theirs = ref.at[laned(at, 1 - core, n)]
         return remote(mine, mine, send, recv, sib), remote(theirs, theirs, send, recv, sib)
 
-    sib_a = [both_ways(ga, k * 6 * R, 3 * R, siba_s.at[k], siba_r.at[k]) for k in range(K)]
+    sib_a = [both_ways(ga, k * 6 * R, 3 * R, siba_s.at[k], siba_r.at[k]) for k in range(K - 1)]
+
+    def last_ways(stream):
+        mine, theirs = (
+            ga.at[pl.ds(pl.multiple_of(((K - 1) * 6 + stream + c * 3) * R, 16), R)] for c in (core, 1 - core)
+        )
+        send, recv = siba_s.at[K - 1 + stream], siba_r.at[K - 1 + stream]
+        return remote(mine, mine, send, recv, sib), remote(theirs, theirs, send, recv, sib)
+
+    sib_last = [last_ways(stream) for stream in range(3)]
     at_1 = [k * 2 * R + (0 if k < 4 else 8 * R) for k in range(K)]
     at_2 = [i * 2 * R2 + (8 * R if i < 8 else 12 * R) for i in range(N2)]
     sib_1 = [both_ways(gb, at_1[k], R, sib1_s.at[k], sib1_r.at[k]) for k in range(K)]
@@ -232,9 +241,14 @@
     p0, p1, p2 = ROWS, ROWS + T, ROWS + 2 * T
 
     def arrive(k):
+        last = k == K - 1
         own_outer[k].wait_recv()
+        if last:
+            sib_last[0][0].start()
         fwd[k].start()
         own_behind[k].wait_recv()
+        if last:
+            sib_last[1][0].start()
         for i in (2 * k, 2 * k + 1):
             if i < NP:
                 rel[i].start()
@@ -242,7 +256,10 @@
             own_pair[4].start()
             own_pair[5].start()
         own_ahead[k].wait_recv()
-        sib_a[k][0].start()
+        if last:
+            sib_last[2][0].start()
+        else:
+            sib_a[k][0].start()
         if k < 4:
             arrive_pair(k)
 
@@ -285,7 +302,8 @@
     pull_a(p0, 2 * T, 4, 1)
     pull_last(p0, 2 * T, core)
     pass_on(4)
-    sib_a[5][1].wait_recv()
+    for _, copy in sib_last:
+        copy.wait_recv()
     pull_last(p0, 2 * T, 1 - core)
     send_partial(0)
     send_partial(1)
@@ -365,7 +383,7 @@
     for copies in (own_pair, own_outer, own_behind, own_ahead, fwd, rel, rel_out, partial[:2], e_copies):
         for copy in copies:
             copy.wait_send()
-    for copies in (sib_a, sib_1, sib_2):
+    for copies in (sib_a, sib_last, sib_1, sib_2):
         for copy, _ in copies:
             copy.wait_send()
     for copy in (e_sib, e_fwd, e_rel, e_out, e_sibb, sib_own, sib_pair):
@@ -409,7 +427,7 @@
                 pltpu.VMEM((8, 6 * ROWS), f32),
                 pltpu.VMEM((8, 4 * ROWS), f32),
                 dma((K,)), dma((2,)), dma((2,)), dma((2,)), dma((4, K)), dma((4, K)),
-                dma((K,)), dma((K,)), dma((K,)), dma((K,)), dma((N2,)), dma((N2,)),
+                dma((K + 2,)), dma((K + 2,)), dma((K,)), dma((K,)), dma((N2,)), dma((N2,)),
                 dma((N2,)), dma((N2,)), dma((K,)), dma((K,)), dma((N2,)), dma((N2,)),
                 dma((len(TILES),)), dma((len(TILES),)), dma((9,)), dma((9,)),
             ],

time: 54.1 us -> 54.2 us (level)
  no operation moved by 1% of the time
where the time goes in v5:
time: 54.2 us; the launch traced here: 54.1 us
  Pallas kernels  52.9 us (98%)
  local copies, waits for them, and re-layouts  1.15 us (2%)
    pallas_call x1, Pallas kernels, per_device(): pl.pallas_call(functools.partial(kernel, blocks), out_shape=jax.ShapeDtyp...  52.9 us
    unnamed x1, local copies, waits for them, and re-layouts  1.15 us

profile of v5, /device:TPU:1, one launch (start us, length us, event | category | flops | bytes accessed | tf_op | source)
XLA Modules:
  0.0 54.1 jit_solution(1174304636841778876)
XLA Ops:
  0.0 52.9 %shard_map.37 = f32[384,1024]{1,0:T(8,128)S(1)} custom-call(f32[384,1024]{1,0:T(8,128)} %emb_hbm.1, bf16[384]{0:T(512)(128)(2,1)} %norm_hbm.1, s32[384]{0:T(512)} %partner_hbm.1), custom_call_target="tpu_custom_call" | custom-call | flops 10000000000 | bytes 4194304 | tf_op jit(solution)/shard_map/pallas_call | solution.py:403
  52.9 1.1 %copy.5 = f32[384,1024]{1,0:T(8,128)} copy(f32[384,1024]{1,0:T(8,128)S(1)} %shard_map.37) | data formatting | bytes 3145728
